TPU v7x, 32 devices: a whole 2x2x4 slice. The times are simulated.
32 devices in a mesh: gx: 8 (over z, y), gy: 4 (over x, core).
Axes of the slice: x: 2, y: 2, z: 4, core: 2. Of those that a mesh axis runs over, the one named last changes fastest.
Arguments:
- flux_perturbation: float32 [2, 4096, 4096], P(None, 'gx', 'gy'), may hold values from -6 to 6
- archived_nominal_heat_levels: float32 [2, 2, 4096, 4096], P(None, None, 'gx', 'gy'), may hold values from -4 to 4
- archived_solidity_labels: int32 [2, 2, 4096, 4096], P(None, None, 'gx', 'gy'), may hold values from 0 to 2
Outputs:
- hess_vec: float32 [2, 4096, 4096], P(None, 'gx', 'gy')
Inputs may be any that keep to these rules, and one draw needn't show every extreme that they name: `archived_solidity_labels`: 0 is solid, 1 mushy, 2 liquid.
All inputs are finite; a program needn't handle non-finite values.
Results may differ from a plain program's by a relative error of at most 0.000061.
Values sent between devices are 32-bit elements; how exact they have to be, the bound alone decides.
A program may use at most 192 MiB of HBM per device.

v0:
```python
import math
import jax
import jax.numpy as jnp
from jax import lax
from jax.sharding import PartitionSpec as P

TIME_STEP = 0.1
OBS_WEIGHT = 10.0
PRIOR_GAIN = 0.005
HIGHEST = lax.Precision.HIGHEST


def with_halo(cells, sides, width):
    for axis, dim in sides:
        count = lax.axis_size(axis)
        ends = count - 1
        head = lax.slice_in_dim(cells, 0, width, axis=dim)
        tail = lax.slice_in_dim(cells, cells.shape[dim] - width, cells.shape[dim], axis=dim)
        cells = jnp.concatenate(
            [
                lax.ppermute(tail, axis, [(i, (i + 1) % count) for i in range(ends)]),
                cells,
                lax.ppermute(head, axis, [((i + 1) % count, i) for i in range(ends)]),
            ],
            axis=dim,
        )
    return cells


def surface_rim(field):
    padded = with_halo(field, (("gx", 1), ("gy", 2)), 1)
    return padded[:, 2:, 1:-1] + padded[:, :-2, 1:-1] + padded[:, 1:-1, 2:] + padded[:, 1:-1, :-2]


def cos_sin(horizontal_line_total, col_count, modulus):
    row_ids = jnp.arange(horizontal_line_total, dtype=jnp.int32)[:, None]
    col_ids = jnp.arange(col_count, dtype=jnp.int32)[None, :]
    angles = (row_ids * col_ids % modulus).astype(jnp.float32) * (2.0 * math.pi / modulus)
    return (jnp.cos(angles), jnp.sin(angles))


def tables(length):
    bit_count = length.bit_length() - 1
    outer_len = 2 ** (bit_count // 2)
    inner_len = length // outer_len
    cos_outer, sin_outer = cos_sin(outer_len, outer_len, outer_len)
    cos_inner, sin_inner = cos_sin(inner_len, inner_len, inner_len)
    twist_cos, twist_sin = cos_sin(outer_len, inner_len, length)
    outer_fwd = jnp.stack([cos_outer, -sin_outer])
    inner_fwd = jnp.stack([jnp.stack([cos_inner, -sin_inner]), jnp.stack([sin_inner, cos_inner])])
    inner_inv = jnp.stack([jnp.stack([cos_inner, sin_inner]), jnp.stack([-sin_inner, cos_inner])])
    outer_inv = jnp.stack([cos_outer, -sin_outer])
    freq_index = (
        jnp.arange(outer_len, dtype=jnp.int32)[:, None]
        + outer_len * jnp.arange(inner_len, dtype=jnp.int32)[None, :]
    )
    signed = jnp.where(freq_index < length // 2, freq_index, freq_index - length).astype(
        jnp.float32
    )
    wave_sq = (signed * (2.0 * math.pi / length)) ** 2
    return (
        length,
        outer_len,
        inner_len,
        outer_fwd,
        inner_fwd,
        inner_inv,
        outer_inv,
        twist_cos,
        twist_sin,
        wave_sq,
    )


def forward(field, table):
    (
        length,
        outer_len,
        inner_len,
        outer_fwd,
        inner_fwd,
        inner_inv,
        outer_inv,
        twist_cos,
        twist_sin,
        wave_sq,
    ) = table
    grid = field.reshape(field.shape[:-1] + (outer_len, inner_len))
    stepped = jnp.einsum("...ab,rak->...rkb", grid, outer_fwd, precision=HIGHEST)
    step_re = stepped[..., 0, :, :]
    step_im = stepped[..., 1, :, :]
    twisted = jnp.stack(
        [step_re * twist_cos + step_im * twist_sin, step_im * twist_cos - step_re * twist_sin],
        axis=-3,
    )
    spec = jnp.einsum("...rkb,rsbm->...skm", twisted, inner_fwd, precision=HIGHEST)
    return (spec[..., 0, :, :], spec[..., 1, :, :])


def inverse(spec_re, spec_im, table):
    (
        length,
        outer_len,
        inner_len,
        outer_fwd,
        inner_fwd,
        inner_inv,
        outer_inv,
        twist_cos,
        twist_sin,
        wave_sq,
    ) = table
    stacked = jnp.stack([spec_re, spec_im], axis=-3)
    halved = jnp.einsum("...skm,srbm->...rkb", stacked, inner_inv, precision=HIGHEST)
    half_re = halved[..., 0, :, :]
    half_im = halved[..., 1, :, :]
    turned = jnp.stack(
        [half_re * twist_cos - half_im * twist_sin, half_im * twist_cos + half_re * twist_sin],
        axis=-3,
    )
    grid = jnp.einsum("...rkb,rka->...ab", turned, outer_inv, precision=HIGHEST)
    return grid.reshape(grid.shape[:-2] + (length,)) / length


def shards(flux_perturbation, archived_nominal_heat_levels, archived_solidity_labels):
    capacity = jnp.where(
        archived_solidity_labels == 0, 1.0, jnp.where(archived_solidity_labels == 1, 4.0, 1.25)
    ).astype(jnp.float32)
    diffusion_advance = jnp.where(
        archived_solidity_labels == 0, 1.0, jnp.where(archived_solidity_labels == 1, 0.6, 0.35)
    ).astype(jnp.float32)
    diffusion_advance = diffusion_advance * (1.0 + 0.5 * jnp.tanh(archived_nominal_heat_levels))
    rows = lax.all_to_all(flux_perturbation, "gx", split_axis=2, concat_axis=1, tiled=True)
    row_table = tables(rows.shape[1])
    first_u = TIME_STEP * flux_perturbation / capacity[0, 0]
    second_top = TIME_STEP * flux_perturbation + TIME_STEP * (
        diffusion_advance[0, 0] * (surface_rim(first_u) - 6.0 * first_u) + flux_perturbation
    )
    second_low = TIME_STEP * diffusion_advance[0, 1] * first_u
    top_u = second_top / capacity[1, 0]
    low_u = second_low / capacity[1, 1]
    third_top = second_top + TIME_STEP * (
        diffusion_advance[1, 0] * (surface_rim(top_u) - 6.0 * top_u + low_u) + flux_perturbation
    )
    misfit = OBS_WEIGHT * third_top / capacity[1, 0]
    adj_three = misfit / capacity[1, 0]
    push_top = TIME_STEP * diffusion_advance[1, 0] * adj_three
    adj_two_top = adj_three + (surface_rim(push_top) - 6.0 * push_top) / capacity[1, 0]
    adj_two_low = push_top / capacity[1, 1]
    pull_top = TIME_STEP * diffusion_advance[0, 0] * adj_two_top
    pull_low = TIME_STEP * diffusion_advance[0, 1] * adj_two_low
    adj_one_top = adj_two_top + (surface_rim(pull_top) - 6.0 * pull_top + pull_low) / capacity[0, 0]
    data_term = TIME_STEP * (adj_three + adj_two_top + adj_one_top)
    row_re, row_im = forward(jnp.swapaxes(rows, 1, 2), row_table)
    wave_x = row_table[-1]
    second_x = jnp.swapaxes(
        inverse(2.0 * PRIOR_GAIN * wave_x * row_re, 2.0 * PRIOR_GAIN * wave_x * row_im, row_table),
        1,
        2,
    )
    fourth_x = jnp.swapaxes(
        inverse(
            PRIOR_GAIN * wave_x * wave_x * row_re, PRIOR_GAIN * wave_x * wave_x * row_im, row_table
        ),
        1,
        2,
    )
    second_back, fourth_part = (
        lax.all_to_all(second_x, "gx", split_axis=1, concat_axis=2, tiled=True),
        lax.all_to_all(fourth_x, "gx", split_axis=1, concat_axis=2, tiled=True),
    )
    cols_dir, cols_second = (
        lax.all_to_all(flux_perturbation, "gy", split_axis=1, concat_axis=2, tiled=True),
        lax.all_to_all(second_back, "gy", split_axis=1, concat_axis=2, tiled=True),
    )
    col_table = tables(cols_dir.shape[2])
    dir_re, dir_im = forward(cols_dir, col_table)
    sec_re, sec_im = forward(cols_second, col_table)
    wave_y = col_table[-1]
    mixed = inverse(
        PRIOR_GAIN * wave_y * wave_y * dir_re + wave_y * sec_re,
        PRIOR_GAIN * wave_y * wave_y * dir_im + wave_y * sec_im,
        col_table,
    )
    mixed_back = lax.all_to_all(mixed, "gy", split_axis=2, concat_axis=1, tiled=True)
    return data_term + fourth_part + mixed_back


def solution(mesh):
    in_specs = (P(None, "gx", "gy"), P(None, None, "gx", "gy"), P(None, None, "gx", "gy"))
    out_specs = P(None, "gx", "gy")
    return jax.shard_map(shards, mesh=mesh, in_specs=in_specs, out_specs=out_specs, check_vma=False)
```

profile of v0, /device:TPU:17, one launch (start us, length us, event | category | flops | bytes accessed | tf_op | source)
XLA Modules:
  0.0 816.4 jit_solution(504303709747888213)
XLA Ops:
  0.0 7.4 copy.232
  12.9 7.2 copy.218
  20.1 40.2 %all-to-all-done.2 = f32[2,512,1024]{2,0,1:T(2,128)} async-done(((f32[2,512,1024]{2,0,1:T(2,128)}), f32[2,512,1024]{2,0,1:T(2,128)}, u32[]{:S(2)}, u32[]{:S(2)}) %all-to-all-start.2) | async-done | bytes 4194336 | tf_op jit(solution)/shard_map/all_to_all | solution.py:173
  60.3 5.8 all-to-all-start
  78.5 13.3 %fusion.81 = f32[2,128,2,64,64]{1,3,4,0,2:T(8,128)} fusion(f32[2,128,64,64]{1,3,2,0:T(8,128)} %bitcast.223, f32[1,64,64]{1,2,0:T(8,128)S(1)} %get-tuple-element.69, f32[1,64,64]{1,2,0:T(8,128)S(1)} %get-tuple-element.70), kind=kOutput, calls=%fused_computation.149 | convolution fusion | flops 1610620928 | bytes 12615680 | tf_op jit(solution)/shard_map/...ab,rak->...rkb/dot_general | solution.py:89
  91.8 63.4 %all-to-all-done = f32[2,512,1024]{1,0,2:T(2,128)} async-done(((f32[2,512,1024]{1,0,2:T(2,128)}), f32[2,512,1024]{1,0,2:T(2,128)}, u32[]{:S(2)}, u32[]{:S(2)}) %all-to-all-start) | async-done | bytes 4194336 | tf_op jit(solution)/shard_map/all_to_all | solution.py:133
  165.6 11.7 %fusion.78 = f32[2,128,2,64,64]{1,3,4,0,2:T(8,128)S(1)} fusion(f32[2,128,64,64]{1,3,2,0:T(8,128)} %bitcast.224, f32[1,64,64]{1,2,0:T(8,128)S(1)} %get-tuple-element.69, f32[1,64,64]{1,2,0:T(8,128)S(1)} %get-tuple-element.70), kind=kOutput, calls=%fused_computation.148 | convolution fusion | flops 1610620928 | bytes 12615680 | tf_op jit(solution)/shard_map/...ab,rak->...rkb/dot_general | solution.py:89
  180.5 12.5 %fusion.87 = f32[2,128,2,64,64]{1,4,3,0,2:T(8,128)S(1)} fusion(f32[2,128,2,64,64]{1,3,4,0,2:T(8,128)S(1)} %pad_maximum_fusion, f32[1,2,64,64]{2,3,1,0:T(8,128)S(1)} %get-tuple-element.61, f32[1,2,64,64]{2,3,1,0:T(8,128)S(1)} %get-tuple-element.64), kind=kOutput, calls=%fused_computation.151 | convolution fusion | flops 3221241856 | bytes 16842752 | tf_op jit(solution)/shard_map/...rkb,rsbm->...skm/dot_general | solution.py:96
  196.6 8.5 %fusion.90 = f32[2,64,2,128,64]{3,1,4,2,0:T(8,128)S(1)} fusion(f32[2,128,1,64,64]{1,4,3,0,2:T(8,128)S(1)} %get-tuple-element.27, f32[2,128,1,64,64]{1,4,3,0,2:T(8,128)S(1)} %get-tuple-element.26, f32[1,2,64,64]{2,3,1,0:T(8,128)S(1)} %get-tuple-element.65, f32[1,2,64,64]{2,3,1,0:T(8,128)S(1)} %get-tuple-element.60), kind=kOutput, calls=%fused_computation.152 | convolution fusion | flops 3223339008 | bytes 16842752 | tf_op jit(solution)/shard_map/...skm,srbm->...rkb/dot_general | solution.py:114
  205.1 8.4 %copy.364 = f32[2,64,2,128,64]{3,4,1,2,0:T(8,128)} copy(f32[2,64,2,128,64]{3,1,4,2,0:T(8,128)S(1)} %fusion.90) | data formatting | bytes 16777216 | tf_op jit(solution)/shard_map/...skm,srbm->...rkb/dot_general | solution.py:114
  213.5 10.7 %fusion.96 = f32[2,64,2,128,64]{3,1,4,2,0:T(8,128)S(1)} fusion(f32[2,128,1,64,64]{1,4,3,0,2:T(8,128)S(1)} %get-tuple-element.38, f32[2,128,1,64,64]{1,4,3,0,2:T(8,128)} %get-tuple-element.39, f32[1,2,64,64]{2,3,1,0:T(8,128)S(1)} %get-tuple-element.65, f32[1,2,64,64]{2,3,1,0:T(8,128)S(1)} %get-tuple-element.60), kind=kOutput, calls=%fused_computation.154 | convolution fusion | flops 3223339008 | bytes 16842752 | tf_op jit(solution)/shard_map/...skm,srbm->...rkb/dot_general | solution.py:114
  224.2 8.5 %copy.363 = f32[2,64,2,128,64]{3,4,1,2,0:T(8,128)} copy(f32[2,64,2,128,64]{3,1,4,2,0:T(8,128)S(1)} %fusion.96) | data formatting | bytes 16777216 | tf_op jit(solution)/shard_map/...skm,srbm->...rkb/dot_general | solution.py:114
  232.7 12.8 %multiply_subtract_fusion.4 = (f32[2,128,1,64,64]{1,3,4,0,2:T(8,128)}, f32[2,128,1,64,64]{1,3,4,0,2:T(8,128)}, f32[2,128,1,64,64]{1,3,4,0,2:T(8,128)}, f32[2,128...) fusion(f32[2,128,2,64,64]{1,3,4,0,2:T(8,128)} %bitcast.221, ...), kind=kLoop, calls=%fused_computation.138 | loop fusion | flops 18874368 | bytes 50364416 | tf_op jit(solution)/shard_map/sub | solution.py:118
  252.9 16.4 %copy.245 = f32[2,4096,128]{2,0,1:T(2,128)} copy(f32[2,4096,128]{2,1,0:T(8,128)S(1)} %bitcast.228) | data formatting | bytes 8388608 | tf_op jit(solution)/shard_map/transpose | solution.py:156
  269.3 8.0 all-to-all-start.3
  282.7 83.3 %all-to-all-done.3 = f32[2,4096,128]{2,0,1:T(2,128)} async-done(((f32[2,4096,128]{2,0,1:T(2,128)}), f32[2,4096,128]{2,0,1:T(2,128)}, u32[]{:S(2)}, u32[]{:S(2)}) %all-to-all-start.3) | async-done | bytes 4194336 | tf_op jit(solution)/shard_map/all_to_all | solution.py:169
  375.9 7.4 copy.248
  383.3 7.3 all-to-all-start.4
  390.5 9.8 %add_multiply_fusion = (f32[2,2,512,1024]{3,2,1,0:T(8,128)}, pred[2,2,512,1024]{3,2,1,0:T(8,128)(4,1)S(1)}, pred[2,2,512,1024]{3,2,1,0:T(8,128)(4,1)S(1)}) fusion(f32[2,2,512,1024]{3,2,1,0:T(8,128)} %param.4, s32[2,2,512,1024]{3,2,1,0:T(8,128)} %param.5), kind=kLoop, calls=%fused_computation.40 | loop fusion | flops 14680064 | bytes 29360128 | tf_op jit(solution)/shard_map/mul | solution.py:132
  423.1 7.3 fusion.67
  432.8 16.2 %copy.229 = f32[2,4096,128]{2,0,1:T(2,128)} copy(f32[2,4096,128]{2,1,0:T(8,128)S(1)} %bitcast.231) | data formatting | bytes 8388608 | tf_op jit(solution)/shard_map/transpose | solution.py:161
  449.0 8.1 all-to-all-start.1
  484.3 14.6 %broadcast_divide_fusion = f32[2,512,1024]{1,2,0:T(8,128)S(1)} fusion(f32[512,1024]{0,1:T(8,128)} %copy.192, f32[2,512,1024]{1,2,0:T(8,128)} %copy.181, f32[2,512,1024]{1,2,0:T(8,128)} %copy-done, f32[2,1,1024]{1,2,0:T(8,128)S(1)} %copy.185, f32[2,1,1024]{1,2,0:T(8,128)} %copy.187, f32[2,514,1]{1,2,0:T(1,128)S(1)} %collective-permute-done.3, ...), kind=kLoop, calls=%fused_computation.166 | loop fusion | flops 19922944 | bytes 16801824 | tf_op jit(solution)/shard_map/div | solution.py:140
  531.5 15.3 %collective-permute-done.4 = f32[2,1,1024]{2,0,1:T(2,128)} collective-permute-done((f32[2,1,1024]{2,0,1:T(2,128)}, f32[2,1,1024]{2,0,1:T(2,128)}, u32[]{:S(2)}, u32[]{:S(2)}) %collective-permute-start.4) | collective-permute-done | bytes 8224 | tf_op jit(solution)/shard_map/ppermute | solution.py:23
  562.7 13.1 %fusion.93 = f32[2,128,2,64,64]{1,4,3,0,2:T(8,128)} fusion(f32[2,128,2,64,64]{1,3,4,0,2:T(8,128)S(1)} %pad_maximum_fusion.2, f32[1,2,64,64]{2,3,1,0:T(8,128)S(1)} %get-tuple-element.61, f32[1,2,64,64]{2,3,1,0:T(8,128)S(1)} %get-tuple-element.64), kind=kOutput, calls=%fused_computation.153 | convolution fusion | flops 3221241856 | bytes 16842752 | tf_op jit(solution)/shard_map/...rkb,rsbm->...skm/dot_general | solution.py:96
  586.6 11.3 %fusion.84 = f32[2,128,2,64,64]{1,3,4,0,2:T(8,128)S(1)} fusion(f32[2,128,64,64]{1,3,2,0:T(8,128)} %bitcast.225, f32[1,64,64]{1,2,0:T(8,128)S(1)} %get-tuple-element.69, f32[1,64,64]{1,2,0:T(8,128)S(1)} %get-tuple-element.70), kind=kOutput, calls=%fused_computation.150 | convolution fusion | flops 1610620928 | bytes 12615680 | tf_op jit(solution)/shard_map/...ab,rak->...rkb/dot_general | solution.py:89
  603.8 15.9 %fusion.99 = f32[2,128,2,64,64]{1,4,3,0,2:T(8,128)S(1)} fusion(f32[2,128,2,64,64]{1,3,4,0,2:T(8,128)} %pad_maximum_fusion.4, f32[1,2,64,64]{2,3,1,0:T(8,128)S(1)} %get-tuple-element.61, f32[1,2,64,64]{2,3,1,0:T(8,128)S(1)} %get-tuple-element.64), kind=kOutput, calls=%fused_computation.155 | convolution fusion | flops 3221241856 | bytes 16842752 | tf_op jit(solution)/shard_map/...rkb,rsbm->...skm/dot_general | solution.py:96
  624.6 10.8 %fusion.102 = f32[2,64,2,128,64]{3,1,4,2,0:T(8,128)S(1)} fusion(f32[2,128,1,64,64]{1,4,3,0,2:T(8,128)} %get-tuple-element.13, f32[2,128,1,64,64]{1,4,3,0,2:T(8,128)} %get-tuple-element.12, f32[1,2,64,64]{2,3,1,0:T(8,128)S(1)} %get-tuple-element.65, f32[1,2,64,64]{2,3,1,0:T(8,128)S(1)} %get-tuple-element.60), kind=kOutput, calls=%fused_computation.156 | convolution fusion | flops 3223339008 | bytes 16842752 | tf_op jit(solution)/shard_map/...skm,srbm->...rkb/dot_general | solution.py:114
  649.5 16.1 %copy.259 = f32[2,128,4096]{1,0,2:T(2,128)} copy(f32[2,128,4096]{1,2,0:T(8,128)S(1)} %bitcast.233) | data formatting | bytes 8388608 | tf_op jit(solution)/shard_map/div | solution.py:122
  670.7 30.2 %broadcast_multiply_fusion.1 = (f32[2,512,1024]{1,2,0:T(8,128)S(1)}, f32[2,512,1024]{1,2,0:T(8,128)}) fusion(f32[512,1024]{0,1:T(8,128)} %copy.203, f32[512,1024]{0,1:T(8,128)} %copy.202, f32[2,512,1024]{1,2,0:T(8,128)} %copy.181, f32[512,1024]{0,1:T(8,128)} %copy.200, f32[512,1024]{0,1:T(8,128)S(1)} %copy.183, f32[512,1024]{0,1:T(8,128)} %copy.199, ...), kind=kLoop, calls=%fused_computation.165 | loop fusion | flops 44040192 | bytes 35700800 | tf_op jit(solution)/shard_map/mul | solution.py:147
  728.9 15.4 %broadcast_multiply_fusion = (f32[2,512,1024]{1,2,0:T(8,128)S(1)}, f32[2,512,1024]{1,2,0:T(8,128)}) fusion(f32[512,1024]{0,1:T(8,128)} %copy.210, f32[2,512,1024]{1,2,0:T(8,128)} %get-tuple-element.8, f32[512,1024]{0,1:T(8,128)} %copy.192, f32[2,512,1024]{1,2,0:T(8,128)} %copy-done.3, f32[2,1,1024]{1,2,0:T(8,128)S(1)} %copy.205, f32[2,1,1024]{1,2,0:T(8,128)} %copy.207, ...), kind=kLoop, calls=%fused_computation.164 | loop fusion | flops 16777216 | bytes 20996128 | tf_op jit(solution)/shard_map/mul | solution.py:150
  791.0 19.8 %fusion.72 = f32[2,512,1024]{1,2,0:T(8,128)} fusion(f32[2,512,1024]{1,2,0:T(8,128)} %copy.262, f32[2,512,8,128]{1,3,2,0:T(8,128)} %copy.231, f32[2,512,1024]{1,2,0:T(8,128)} %get-tuple-element.6, f32[2,512,1024]{1,2,0:T(8,128)} %copy-done.2, f32[2,1,1024]{1,2,0:T(8,128)S(1)} %copy.212, f32[2,1,1024]{1,2,0:T(8,128)} %copy.214, ...), kind=kLoop, calls=%fused_computation.123 | loop fusion | flops 25165824 | bytes 33579040 | tf_op jit(solution)/shard_map/add | solution.py:186
  (141 shorter events, 278.7 us)
Async XLA Ops:
  7.4 52.9 %all-to-all-start.2 = ((f32[2,512,1024]{2,0,1:T(2,128)}), f32[2,512,1024]{2,0,1:T(2,128)}, u32[]{:S(2)}, u32[]{:S(2)}) async-start(f32[2,512,1024]{2,0,1:T(2,128)} %copy.232), calls=%async_computation.2 | async-start | bytes 8388608 | tf_op jit(solution)/shard_map/all_to_all | solution.py:173
  60.3 94.9 %all-to-all-start = ((f32[2,512,1024]{1,0,2:T(2,128)}), f32[2,512,1024]{1,0,2:T(2,128)}, u32[]{:S(2)}, u32[]{:S(2)}) async-start(f32[2,512,1024]{1,0,2:T(2,128)} %copy.218), calls=%async_computation | async-start | bytes 8388608 | tf_op jit(solution)/shard_map/all_to_all | solution.py:133
  67.0 126.1 %copy-start.6 = (f32[64,64]{1,0:T(8,128)}, f32[64,64]{1,0:T(8,128)S(1)}, u32[]{:S(2)}) copy-start(f32[64,64]{1,0:T(8,128)S(1)} %copy.217) | copy-start | bytes 49156
  205.1 27.6 %slice-start.2 = ((s8[8388608]{0:T(1024)(128)(4,1)}), s8[4194304]{0:T(1024)(128)(4,1)S(1)}, s32[]{:S(2)}) async-start(s8[8388608]{0:T(1024)(128)(4,1)} %bitcast.219), calls=%async_computation.8 | async-start | bytes 8388608
  213.5 19.3 %slice-start.3 = ((s8[8388608]{0:T(1024)(128)(4,1)}), s8[4194304]{0:T(1024)(128)(4,1)S(1)}, s32[]{:S(2)}) async-start(s8[8388608]{0:T(1024)(128)(4,1)} %bitcast.219), calls=%async_computation.9 | async-start | bytes 8388608
  269.3 96.7 %all-to-all-start.3 = ((f32[2,4096,128]{2,0,1:T(2,128)}), f32[2,4096,128]{2,0,1:T(2,128)}, u32[]{:S(2)}, u32[]{:S(2)}) async-start(f32[2,4096,128]{2,0,1:T(2,128)} %copy.245), calls=%async_computation.3 | async-start | bytes 8388608 | tf_op jit(solution)/shard_map/all_to_all | solution.py:169
  383.3 65.7 %all-to-all-start.4 = ((f32[2,512,1024]{2,0,1:T(2,128)}), f32[2,512,1024]{2,0,1:T(2,128)}, u32[]{:S(2)}, u32[]{:S(2)}) async-start(f32[2,512,1024]{2,0,1:T(2,128)} %copy.248), calls=%async_computation.4 | async-start | bytes 8388608 | tf_op jit(solution)/shard_map/all_to_all | solution.py:174
  401.9 5.1 copy-start.4
  416.9 46.0 %collective-permute-start = (f32[2,1,1024]{2,0,1:T(2,128)S(1)}, f32[2,1,1024]{2,0,1:T(2,128)S(1)}, u32[]{:S(2)}, u32[]{:S(2)}) collective-permute-start(f32[2,1,1024]{2,0,1:T(2,128)S(1)} %copy.184), channel_id=1, source_target_pairs={{4,0},{8,4},{12,8},{16,12},{20,16},{24,20},{28,24},{5,1},{9,5},{13... | collective-permute-start | bytes 24584 | tf_op jit(solution)/shard_map/ppermute | solution.py:23
  420.9 42.4 %collective-permute-start.1 = (f32[2,1,1024]{2,0,1:T(2,128)}, f32[2,1,1024]{2,0,1:T(2,128)}, u32[]{:S(2)}, u32[]{:S(2)}) collective-permute-start(f32[2,1,1024]{2,0,1:T(2,128)} %copy.186), channel_id=1, source_target_pairs={{0,4},{4,8},{8,12},{12,16},{16,20},{20,24},{24,28},{1,5},{5,9},{9,... | collective-permute-start | bytes 24584 | tf_op jit(solution)/shard_map/ppermute | solution.py:21
  449.0 216.7 %all-to-all-start.1 = ((f32[2,4096,128]{2,0,1:T(2,128)}), f32[2,4096,128]{2,0,1:T(2,128)}, u32[]{:S(2)}, u32[]{:S(2)}) async-start(f32[2,4096,128]{2,0,1:T(2,128)} %copy.229), calls=%async_computation.1 | async-start | bytes 8388608 | tf_op jit(solution)/shard_map/all_to_all | solution.py:170
  466.9 17.4 %collective-permute-start.3 = (f32[2,514,1]{1,2,0:T(1,128)}, f32[2,514,1]{1,2,0:T(1,128)S(1)}, u32[]{:S(2)}, u32[]{:S(2)}) collective-permute-start(f32[2,514,1]{1,2,0:T(1,128)} %get-tuple-element.47), channel_id=1, source_target_pairs={{0,1},{1,2},{2,3},{4,5},{5,6},{6,7},{8,9},{9,10},{10,11},{12,13},{... | collective-permute-start | bytes 12344 | tf_op jit(solution)/shard_map/ppermute | solution.py:21
  471.2 13.0 %collective-permute-start.2 = (f32[2,514,1]{1,2,0:T(1,128)}, f32[2,514,1]{1,2,0:T(1,128)S(1)}, u32[]{:S(2)}, u32[]{:S(2)}) collective-permute-start(f32[2,514,1]{1,2,0:T(1,128)} %get-tuple-element.46), channel_id=1, source_target_pairs={{1,0},{2,1},{3,2},{5,4},{6,5},{7,6},{9,8},{10,9},{11,10},{13,12},{... | collective-permute-start | bytes 12344 | tf_op jit(solution)/shard_map/ppermute | solution.py:23
  498.9 2.1 copy-start.1
  504.8 42.1 %collective-permute-start.4 = (f32[2,1,1024]{2,0,1:T(2,128)}, f32[2,1,1024]{2,0,1:T(2,128)}, u32[]{:S(2)}, u32[]{:S(2)}) collective-permute-start(f32[2,1,1024]{2,0,1:T(2,128)} %copy.193), channel_id=1, source_target_pairs={{4,0},{8,4},{12,8},{16,12},{20,16},{24,20},{28,24},{5,1},{9,5},{13... | collective-permute-start | bytes 24584 | tf_op jit(solution)/shard_map/ppermute | solution.py:23
  510.0 39.5 %collective-permute-start.5 = (f32[2,1,1024]{2,0,1:T(2,128)}, f32[2,1,1024]{2,0,1:T(2,128)}, u32[]{:S(2)}, u32[]{:S(2)}) collective-permute-start(f32[2,1,1024]{2,0,1:T(2,128)} %copy.195), channel_id=1, source_target_pairs={{0,4},{4,8},{8,12},{12,16},{16,20},{20,24},{24,28},{1,5},{5,9},{9,... | collective-permute-start | bytes 24584 | tf_op jit(solution)/shard_map/ppermute | solution.py:21
  551.6 7.6 copy-start.5
  553.2 117.5 %collective-permute-start.7 = (f32[2,514,1]{1,2,0:T(1,128)}, f32[2,514,1]{1,2,0:T(1,128)}, u32[]{:S(2)}, u32[]{:S(2)}) collective-permute-start(f32[2,514,1]{1,2,0:T(1,128)} %get-tuple-element.45), channel_id=1, source_target_pairs={{0,1},{1,2},{2,3},{4,5},{5,6},{6,7},{8,9},{9,10},{10,11},{12,13},{... | collective-permute-start | bytes 12344 | tf_op jit(solution)/shard_map/ppermute | solution.py:21
  557.3 113.4 %collective-permute-start.6 = (f32[2,514,1]{1,2,0:T(1,128)}, f32[2,514,1]{1,2,0:T(1,128)}, u32[]{:S(2)}, u32[]{:S(2)}) collective-permute-start(f32[2,514,1]{1,2,0:T(1,128)} %get-tuple-element.44), channel_id=1, source_target_pairs={{1,0},{2,1},{3,2},{5,4},{6,5},{7,6},{9,8},{10,9},{11,10},{13,12},{... | collective-permute-start | bytes 12344 | tf_op jit(solution)/shard_map/ppermute | solution.py:23
  599.7 20.1 %slice-start = ((s8[8388608]{0:T(1024)(128)(4,1)}), s8[4194304]{0:T(1024)(128)(4,1)S(1)}, s32[]{:S(2)}) async-start(s8[8388608]{0:T(1024)(128)(4,1)} %bitcast.216), calls=%async_computation.6 | async-start | bytes 8388608
  603.8 16.0 %slice-start.1 = ((s8[8388608]{0:T(1024)(128)(4,1)}), s8[4194304]{0:T(1024)(128)(4,1)S(1)}, s32[]{:S(2)}) async-start(s8[8388608]{0:T(1024)(128)(4,1)} %bitcast.216), calls=%async_computation.7 | async-start | bytes 8388608
  603.8 16.0 %copy-start.7 = (f32[64,64]{1,0:T(8,128)S(1)}, f32[64,64]{1,0:T(8,128)}, u32[]{:S(2)}) copy-start(f32[64,64]{1,0:T(8,128)} %copy-done.6) | copy-start | bytes 49156
  603.8 16.0 %copy-start.8 = (f32[64,64]{1,0:T(8,128)S(1)}, f32[64,64]{1,0:T(8,128)}, u32[]{:S(2)}) copy-start(f32[64,64]{1,0:T(8,128)} %copy.238) | copy-start | bytes 49156
  665.7 110.1 %all-to-all-start.5 = ((f32[2,128,4096]{1,0,2:T(2,128)}), f32[2,128,4096]{1,0,2:T(2,128)}, u32[]{:S(2)}, u32[]{:S(2)}) async-start(f32[2,128,4096]{1,0,2:T(2,128)} %copy.259), calls=%async_computation.5 | async-start | bytes 8388608 | tf_op jit(solution)/shard_map/all_to_all | solution.py:185
  705.9 7.4 collective-permute-start.8
  711.3 5.3 collective-permute-start.9
  718.9 9.9 %collective-permute-start.11 = (f32[2,514,1]{1,2,0:T(1,128)S(1)}, f32[2,514,1]{1,2,0:T(1,128)S(1)}, u32[]{:S(2)}, u32[]{:S(2)}) collective-permute-start(f32[2,514,1]{1,2,0:T(1,128)S(1)} %get-tuple-element.43), channel_id=1, source_target_pairs={{0,1},{1,2},{2,3},{4,5},{5,6},{6,7},{8,9},{9,10},{10,11},{12,13},{... | collective-permute-start | bytes 12344 | tf_op jit(solution)/shard_map/ppermute | solution.py:21
  724.0 4.9 collective-permute-start.10
  749.2 5.6 collective-permute-start.12
  751.5 5.3 collective-permute-start.13
  759.0 31.9 %collective-permute-start.15 = (f32[2,514,1]{1,2,0:T(1,128)S(1)}, f32[2,514,1]{1,2,0:T(1,128)S(1)}, u32[]{:S(2)}, u32[]{:S(2)}) collective-permute-start(f32[2,514,1]{1,2,0:T(1,128)S(1)} %get-tuple-element.41), channel_id=1, source_target_pairs={{0,1},{1,2},{2,3},{4,5},{5,6},{6,7},{8,9},{9,10},{10,11},{12,13},{... | collective-permute-start | bytes 12344 | tf_op jit(solution)/shard_map/ppermute | solution.py:21
  763.7 27.2 %collective-permute-start.14 = (f32[2,514,1]{1,2,0:T(1,128)S(1)}, f32[2,514,1]{1,2,0:T(1,128)S(1)}, u32[]{:S(2)}, u32[]{:S(2)}) collective-permute-start(f32[2,514,1]{1,2,0:T(1,128)S(1)} %get-tuple-element.40), channel_id=1, source_target_pairs={{1,0},{2,1},{3,2},{5,4},{6,5},{7,6},{9,8},{10,9},{11,10},{13,12},{... | collective-permute-start | bytes 12344 | tf_op jit(solution)/shard_map/ppermute | solution.py:23
  (3 other events, 6.0 us)
where the time goes:
time: 823 us; the launch traced here: 816 us
  local copies, waits for them, and re-layouts  244 us (30%)
  waiting for transfers between devices  208 us (25%)
  other arithmetic  150 us (18%)
  matrix products  125 us (15%)
  starting transfers between devices  88.5 us (11%)
    all_to_all x1, waiting for transfers between devices, shards(): lax.all_to_all(second_x, 'gx', split_axis=1, concat_axis=2, tiled=True)  83.3 us
    all_to_all x1, waiting for transfers between devices, shards(): lax.all_to_all(flux_perturbation, 'gx', split_axis=2, concat_axis=1, tile...  63.4 us
    dot_general x3, matrix products, forward(): jnp.einsum('...rkb,rsbm->...skm', twisted, inner_fwd, precision=HIGHEST)  41.5 us
    all_to_all x1, waiting for transfers between devices, shards(): lax.all_to_all(flux_perturbation, 'gy', split_axis=1, concat_axis=2, tile...  40.2 us
    dot_general x3, matrix products, forward(): jnp.einsum('...ab,rak->...rkb', grid, outer_fwd, precision=HIGHEST)  36.2 us
    mul x2, other arithmetic, shards(): push_top = TIME_STEP * diffusion_advance[1, 0] * adj_three  35.4 us
    unnamed x29, local copies, waits for them, and re-layouts  30.3 us
    dot_general x3, matrix products, inverse(): jnp.einsum('...skm,srbm->...rkb', stacked, inner_inv, precision=HIGHEST)  30 us
  transfers between devices with their start and end apart: 22, of which 8 were waited for; matrix products, arithmetic and copies ran while one was open for 42% of the time, Pallas kernels for 0%

commit v1 on v0

--- a/solution.py
+++ b/solution.py
@@ -8,6 +8,28 @@
 OBS_WEIGHT = 10.0
 PRIOR_GAIN = 0.005
 HIGHEST = lax.Precision.HIGHEST
+
+
+def split_up(x, dim, count):
+    before, after = (x.shape[:dim], x.shape[dim + 1 :])
+    return jnp.moveaxis(x.reshape(*before, count, -1, *after), dim, 0)
+
+
+def in_order(blocks, dim):
+    dims = list(blocks.shape[1:])
+    dims[dim] *= blocks.shape[0]
+    return jnp.moveaxis(blocks, 0, dim).reshape(dims)
+
+
+def pairwise_exchange(shard, axis, split_dim, concat_dim):
+    size, position = (lax.axis_size(axis), lax.axis_index(axis))
+    pieces = split_up(shard, split_dim, size)
+    outs = [pieces[position]]
+    for turn in range(1, size):
+        sent = pieces[position ^ turn]
+        outs.append(lax.ppermute(sent, axis, [(i, i ^ turn) for i in range(size)]))
+    pieces = jnp.stack(outs)[position ^ jnp.arange(size)]
+    return in_order(pieces, concat_dim)
 
 
 def with_halo(cells, sides, width):
@@ -170,7 +192,7 @@
         lax.all_to_all(fourth_x, "gx", split_axis=1, concat_axis=2, tiled=True),
     )
     cols_dir, cols_second = (
-        lax.all_to_all(flux_perturbation, "gy", split_axis=1, concat_axis=2, tiled=True),
+        pairwise_exchange(flux_perturbation, "gy", 1, 2),
         lax.all_to_all(second_back, "gy", split_axis=1, concat_axis=2, tiled=True),
     )
     col_table = tables(cols_dir.shape[2])

time: 823 us -> 771 us (0.937)
  waiting for transfers between devices: 208 us -> 156 us
    all_to_all x1, waiting for transfers between devices: 63.4 us -> 8.69 us  [shards(): lax.all_to_all(flux_perturbation, 'gx', split_axis=2, concat_axis=1, tile...]
    ppermute x0 -> x3, waiting for transfers between devices: none -> 43.7 us  [pairwise_exchange(): outs.append(lax.ppermute(sent, axis, [(i, i ^ turn) for i in range(size)]))]
    all_to_all x1 -> x0, waiting for transfers between devices: 40.2 us -> none  [shards(): lax.all_to_all(flux_perturbation, 'gy', split_axis=1, concat_axis=2, tile...]
    all_to_all x2 -> x0, local copies, waits for them, and re-layouts: 10.9 us -> none  [shards(): lax.all_to_all(flux_perturbation, 'gy', split_axis=1, concat_axis=2, tile...]
    unnamed x29 -> x30, local copies, waits for them, and re-layouts: 30.3 us -> 22.7 us
  transfers between devices with their start and end apart: 22 -> 24, of which waited for: 8 -> 9; matrix products, arithmetic and copies ran while one was open for 42% -> 45% of each run, Pallas kernels for 0% -> 0%
where the time goes in v1:
time: 771 us; the launch traced here: 762 us
  local copies, waits for them, and re-layouts  241 us (31%)
  waiting for transfers between devices  156 us (20%)
  other arithmetic  154 us (20%)
  matrix products  125 us (16%)
  starting transfers between devices  85.3 us (11%)
    all_to_all x1, waiting for transfers between devices, shards(): lax.all_to_all(second_x, 'gx', split_axis=1, concat_axis=2, tiled=True)  83.3 us
    ppermute x3, waiting for transfers between devices, pairwise_exchange(): outs.append(lax.ppermute(sent, axis, [(i, i ^ turn) for i in range(size)]))  43.7 us
    dot_general x3, matrix products, forward(): jnp.einsum('...rkb,rsbm->...skm', twisted, inner_fwd, precision=HIGHEST)  42 us
    dot_general x3, matrix products, forward(): jnp.einsum('...ab,rak->...rkb', grid, outer_fwd, precision=HIGHEST)  36 us
    mul x2, other arithmetic, shards(): push_top = TIME_STEP * diffusion_advance[1, 0] * adj_three  35.1 us
    dot_general x3, matrix products, inverse(): jnp.einsum('...skm,srbm->...rkb', stacked, inner_inv, precision=HIGHEST)  29.8 us
    ppermute x8, starting transfers between devices, with_halo(): lax.ppermute(tail, axis, [(i, (i + 1) % count) for i in range(ends)])  27.9 us
    div x4, local copies, waits for them, and re-layouts, inverse(): return grid.reshape(grid.shape[:-2] + (length,)) / length  23.4 us
  transfers between devices with their start and end apart: 24, of which 9 were waited for; matrix products, arithmetic and copies ran while one was open for 45% of the time, Pallas kernels for 0%

profile of v1, /device:TPU:17, one launch (start us, length us, event | category | flops | bytes accessed | tf_op | source)
XLA Modules:
  0.0 761.9 jit_solution(8609543655886416063)
XLA Ops:
  0.0 7.2 copy.224
  21.7 21.3 %collective-permute-done.18 = f32[2,128,1024]{2,1,0:T(8,128)} collective-permute-done((f32[2,128,1024]{2,1,0:T(8,128)}, f32[2,128,1024]{2,1,0:T(8,128)}, u32[]{:S(2)}, u32[]{:S(2)}) %collective-permute-start.18) | collective-permute-done | bytes 1048608 | tf_op jit(solution)/shard_map/ppermute | solution.py:30
  43.0 22.4 %collective-permute-done.17 = f32[2,128,1024]{2,1,0:T(8,128)} collective-permute-done((f32[2,128,1024]{2,1,0:T(8,128)S(1)}, f32[2,128,1024]{2,1,0:T(8,128)}, u32[]{:S(2)}, u32[]{:S(2)}) %collective-permute-start.17) | collective-permute-done | bytes 1048608 | tf_op jit(solution)/shard_map/ppermute | solution.py:30
  80.1 13.3 %fusion.81 = f32[2,128,2,64,64]{1,3,4,0,2:T(8,128)} fusion(f32[2,128,64,64]{1,3,2,0:T(8,128)} %bitcast.244, f32[1,64,64]{1,2,0:T(8,128)S(1)} %get-tuple-element.73, f32[1,64,64]{1,2,0:T(8,128)S(1)} %get-tuple-element.74), kind=kOutput, calls=%fused_computation.151 | convolution fusion | flops 1610620928 | bytes 12615680 | tf_op jit(solution)/shard_map/...ab,rak->...rkb/dot_general | solution.py:111
  93.4 8.7 %all-to-all-done = f32[2,512,1024]{1,0,2:T(2,128)} async-done(((f32[2,512,1024]{1,0,2:T(2,128)}), f32[2,512,1024]{1,0,2:T(2,128)}, u32[]{:S(2)}, u32[]{:S(2)}) %all-to-all-start) | async-done | bytes 4194336 | tf_op jit(solution)/shard_map/all_to_all | solution.py:155
  112.5 11.4 %fusion.78 = f32[2,128,2,64,64]{1,3,4,0,2:T(8,128)S(1)} fusion(f32[2,128,64,64]{1,3,2,0:T(8,128)} %bitcast.245, f32[1,64,64]{1,2,0:T(8,128)S(1)} %get-tuple-element.73, f32[1,64,64]{1,2,0:T(8,128)S(1)} %get-tuple-element.74), kind=kOutput, calls=%fused_computation.150 | convolution fusion | flops 1610620928 | bytes 12615680 | tf_op jit(solution)/shard_map/...ab,rak->...rkb/dot_general | solution.py:111
  127.2 12.8 %fusion.87 = f32[2,128,2,64,64]{1,4,3,0,2:T(8,128)S(1)} fusion(f32[2,128,2,64,64]{1,3,4,0,2:T(8,128)S(1)} %pad_maximum_fusion, f32[1,2,64,64]{2,3,1,0:T(8,128)S(1)} %get-tuple-element.65, f32[1,2,64,64]{2,3,1,0:T(8,128)S(1)} %get-tuple-element.68), kind=kOutput, calls=%fused_computation.153 | convolution fusion | flops 3221241856 | bytes 16842752 | tf_op jit(solution)/shard_map/...rkb,rsbm->...skm/dot_general | solution.py:118
  143.5 8.5 %fusion.90 = f32[2,64,2,128,64]{3,1,4,2,0:T(8,128)S(1)} fusion(f32[2,128,1,64,64]{1,4,3,0,2:T(8,128)S(1)} %get-tuple-element.27, f32[2,128,1,64,64]{1,4,3,0,2:T(8,128)S(1)} %get-tuple-element.26, f32[1,2,64,64]{2,3,1,0:T(8,128)S(1)} %get-tuple-element.69, f32[1,2,64,64]{2,3,1,0:T(8,128)S(1)} %get-tuple-element.64), kind=kOutput, calls=%fused_computation.154 | convolution fusion | flops 3223339008 | bytes 16842752 | tf_op jit(solution)/shard_map/...skm,srbm->...rkb/dot_general | solution.py:136
  152.0 8.4 %copy.376 = f32[2,64,2,128,64]{3,4,1,2,0:T(8,128)} copy(f32[2,64,2,128,64]{3,1,4,2,0:T(8,128)S(1)} %fusion.90) | data formatting | bytes 16777216 | tf_op jit(solution)/shard_map/...skm,srbm->...rkb/dot_general | solution.py:136
  160.4 10.7 %fusion.96 = f32[2,64,2,128,64]{3,1,4,2,0:T(8,128)S(1)} fusion(f32[2,128,1,64,64]{1,4,3,0,2:T(8,128)S(1)} %get-tuple-element.38, f32[2,128,1,64,64]{1,4,3,0,2:T(8,128)} %get-tuple-element.39, f32[1,2,64,64]{2,3,1,0:T(8,128)S(1)} %get-tuple-element.69, f32[1,2,64,64]{2,3,1,0:T(8,128)S(1)} %get-tuple-element.64), kind=kOutput, calls=%fused_computation.156 | convolution fusion | flops 3223339008 | bytes 16842752 | tf_op jit(solution)/shard_map/...skm,srbm->...rkb/dot_general | solution.py:136
  171.1 8.3 %copy.375 = f32[2,64,2,128,64]{3,4,1,2,0:T(8,128)} copy(f32[2,64,2,128,64]{3,1,4,2,0:T(8,128)S(1)} %fusion.96) | data formatting | bytes 16777216 | tf_op jit(solution)/shard_map/...skm,srbm->...rkb/dot_general | solution.py:136
  179.5 12.8 %multiply_subtract_fusion.4 = (f32[2,128,1,64,64]{1,3,4,0,2:T(8,128)}, f32[2,128,1,64,64]{1,3,4,0,2:T(8,128)}, f32[2,128,1,64,64]{1,3,4,0,2:T(8,128)}, f32[2,128...) fusion(f32[2,128,2,64,64]{1,3,4,0,2:T(8,128)} %bitcast.242, ...), kind=kLoop, calls=%fused_computation.140 | loop fusion | flops 18874368 | bytes 50364416 | tf_op jit(solution)/shard_map/sub | solution.py:140
  199.6 16.7 %copy.253 = f32[2,4096,128]{2,0,1:T(2,128)} copy(f32[2,4096,128]{2,1,0:T(8,128)S(1)} %bitcast.249) | data formatting | bytes 8388608 | tf_op jit(solution)/shard_map/transpose | solution.py:178
  216.3 7.8 %all-to-all-start.2 = ((f32[2,4096,128]{2,0,1:T(2,128)}), f32[2,4096,128]{2,0,1:T(2,128)}, u32[]{:S(2)}, u32[]{:S(2)}) async-start(f32[2,4096,128]{2,0,1:T(2,128)} %copy.253), calls=%async_computation.2 | async-start | bytes 8388608 | tf_op jit(solution)/shard_map/all_to_all | solution.py:191
  229.5 83.3 %all-to-all-done.2 = f32[2,4096,128]{2,0,1:T(2,128)} async-done(((f32[2,4096,128]{2,0,1:T(2,128)}), f32[2,4096,128]{2,0,1:T(2,128)}, u32[]{:S(2)}, u32[]{:S(2)}) %all-to-all-start.2) | async-done | bytes 4194336 | tf_op jit(solution)/shard_map/all_to_all | solution.py:191
  322.6 7.4 copy.256
  330.1 7.3 all-to-all-start.3
  337.3 9.8 %add_multiply_fusion = (f32[2,2,512,1024]{3,2,1,0:T(8,128)}, pred[2,2,512,1024]{3,2,1,0:T(8,128)(4,1)S(1)}, pred[2,2,512,1024]{3,2,1,0:T(8,128)(4,1)S(1)}) fusion(f32[2,2,512,1024]{3,2,1,0:T(8,128)} %param.4, s32[2,2,512,1024]{3,2,1,0:T(8,128)} %param.5), kind=kLoop, calls=%fused_computation.41 | loop fusion | flops 14680064 | bytes 29360128 | tf_op jit(solution)/shard_map/mul | solution.py:154
  369.9 7.1 fusion.67
  379.4 16.2 %copy.235 = f32[2,4096,128]{2,0,1:T(2,128)} copy(f32[2,4096,128]{2,1,0:T(8,128)S(1)} %bitcast.252) | data formatting | bytes 8388608 | tf_op jit(solution)/shard_map/transpose | solution.py:183
  395.6 8.1 %all-to-all-start.1 = ((f32[2,4096,128]{2,0,1:T(2,128)}), f32[2,4096,128]{2,0,1:T(2,128)}, u32[]{:S(2)}, u32[]{:S(2)}) async-start(f32[2,4096,128]{2,0,1:T(2,128)} %copy.235), calls=%async_computation.1 | async-start | bytes 8388608 | tf_op jit(solution)/shard_map/all_to_all | solution.py:192
  403.7 6.0 slice_bitcast_fusion.2
  431.1 14.5 %broadcast_divide_fusion = f32[2,512,1024]{1,2,0:T(8,128)S(1)} fusion(f32[512,1024]{0,1:T(8,128)} %copy.198, f32[2,512,1024]{1,2,0:T(8,128)} %copy.187, f32[2,512,1024]{1,2,0:T(8,128)} %copy-done, f32[2,1,1024]{1,2,0:T(8,128)S(1)} %copy.191, f32[2,1,1024]{1,2,0:T(8,128)} %copy.193, f32[2,514,1]{1,2,0:T(1,128)S(1)} %collective-permute-done.3, ...), kind=kLoop, calls=%fused_computation.168 | loop fusion | flops 19922944 | bytes 16801824 | tf_op jit(solution)/shard_map/div | solution.py:162
  478.3 15.2 %collective-permute-done.4 = f32[2,1,1024]{2,0,1:T(2,128)} collective-permute-done((f32[2,1,1024]{2,0,1:T(2,128)}, f32[2,1,1024]{2,0,1:T(2,128)}, u32[]{:S(2)}, u32[]{:S(2)}) %collective-permute-start.4) | collective-permute-done | bytes 8224 | tf_op jit(solution)/shard_map/ppermute | solution.py:45
  509.3 13.3 %fusion.93 = f32[2,128,2,64,64]{1,4,3,0,2:T(8,128)} fusion(f32[2,128,2,64,64]{1,3,4,0,2:T(8,128)S(1)} %pad_maximum_fusion.2, f32[1,2,64,64]{2,3,1,0:T(8,128)S(1)} %get-tuple-element.65, f32[1,2,64,64]{2,3,1,0:T(8,128)S(1)} %get-tuple-element.68), kind=kOutput, calls=%fused_computation.155 | convolution fusion | flops 3221241856 | bytes 16842752 | tf_op jit(solution)/shard_map/...rkb,rsbm->...skm/dot_general | solution.py:118
  533.5 11.3 %fusion.84 = f32[2,128,2,64,64]{1,3,4,0,2:T(8,128)S(1)} fusion(f32[2,128,64,64]{1,3,2,0:T(8,128)} %bitcast.246, f32[1,64,64]{1,2,0:T(8,128)S(1)} %get-tuple-element.73, f32[1,64,64]{1,2,0:T(8,128)S(1)} %get-tuple-element.74), kind=kOutput, calls=%fused_computation.152 | convolution fusion | flops 1610620928 | bytes 12615680 | tf_op jit(solution)/shard_map/...ab,rak->...rkb/dot_general | solution.py:111
  550.6 15.9 %fusion.99 = f32[2,128,2,64,64]{1,4,3,0,2:T(8,128)S(1)} fusion(f32[2,128,2,64,64]{1,3,4,0,2:T(8,128)} %pad_maximum_fusion.4, f32[1,2,64,64]{2,3,1,0:T(8,128)S(1)} %get-tuple-element.65, f32[1,2,64,64]{2,3,1,0:T(8,128)S(1)} %get-tuple-element.68), kind=kOutput, calls=%fused_computation.157 | convolution fusion | flops 3221241856 | bytes 16842752 | tf_op jit(solution)/shard_map/...rkb,rsbm->...skm/dot_general | solution.py:118
  571.4 10.6 %fusion.102 = f32[2,64,2,128,64]{3,1,4,2,0:T(8,128)S(1)} fusion(f32[2,128,1,64,64]{1,4,3,0,2:T(8,128)} %get-tuple-element.13, f32[2,128,1,64,64]{1,4,3,0,2:T(8,128)} %get-tuple-element.12, f32[1,2,64,64]{2,3,1,0:T(8,128)S(1)} %get-tuple-element.69, f32[1,2,64,64]{2,3,1,0:T(8,128)S(1)} %get-tuple-element.64), kind=kOutput, calls=%fused_computation.158 | convolution fusion | flops 3223339008 | bytes 16842752 | tf_op jit(solution)/shard_map/...skm,srbm->...rkb/dot_general | solution.py:136
  596.3 16.1 %copy.267 = f32[2,128,4096]{1,0,2:T(2,128)} copy(f32[2,128,4096]{1,2,0:T(8,128)S(1)} %bitcast.254) | data formatting | bytes 8388608 | tf_op jit(solution)/shard_map/div | solution.py:144
  617.5 29.9 %broadcast_multiply_fusion.1 = (f32[2,512,1024]{1,2,0:T(8,128)S(1)}, f32[2,512,1024]{1,2,0:T(8,128)}) fusion(f32[512,1024]{0,1:T(8,128)} %copy.209, f32[512,1024]{0,1:T(8,128)} %copy.208, f32[2,512,1024]{1,2,0:T(8,128)} %copy.187, f32[512,1024]{0,1:T(8,128)} %copy.206, f32[512,1024]{0,1:T(8,128)S(1)} %copy.189, f32[512,1024]{0,1:T(8,128)} %copy.205, ...), kind=kLoop, calls=%fused_computation.167 | loop fusion | flops 44040192 | bytes 35700800 | tf_op jit(solution)/shard_map/mul | solution.py:169
  675.3 15.0 %broadcast_multiply_fusion = (f32[2,512,1024]{1,2,0:T(8,128)S(1)}, f32[2,512,1024]{1,2,0:T(8,128)}) fusion(f32[512,1024]{0,1:T(8,128)} %copy.216, f32[2,512,1024]{1,2,0:T(8,128)} %get-tuple-element.8, f32[512,1024]{0,1:T(8,128)} %copy.198, f32[2,512,1024]{1,2,0:T(8,128)} %copy-done.3, f32[2,1,1024]{1,2,0:T(8,128)S(1)} %copy.211, f32[2,1,1024]{1,2,0:T(8,128)} %copy.213, ...), kind=kLoop, calls=%fused_computation.166 | loop fusion | flops 16777216 | bytes 20996128 | tf_op jit(solution)/shard_map/mul | solution.py:172
  736.9 19.4 %fusion.72 = f32[2,512,1024]{1,2,0:T(8,128)} fusion(f32[2,512,1024]{1,2,0:T(8,128)} %copy.270, f32[2,512,8,128]{1,3,2,0:T(8,128)} %copy.237, f32[2,512,1024]{1,2,0:T(8,128)} %get-tuple-element.6, f32[2,512,1024]{1,2,0:T(8,128)} %copy-done.2, f32[2,1,1024]{1,2,0:T(8,128)S(1)} %copy.218, f32[2,1,1024]{1,2,0:T(8,128)} %copy.220, ...), kind=kLoop, calls=%fused_computation.125 | loop fusion | flops 25165824 | bytes 33579040 | tf_op jit(solution)/shard_map/add | solution.py:208
  (150 shorter events, 284.4 us)
Async XLA Ops:
  7.2 94.9 %all-to-all-start = ((f32[2,512,1024]{1,0,2:T(2,128)}), f32[2,512,1024]{1,0,2:T(2,128)}, u32[]{:S(2)}, u32[]{:S(2)}) async-start(f32[2,512,1024]{1,0,2:T(2,128)} %copy.224), calls=%async_computation | async-start | bytes 8388608 | tf_op jit(solution)/shard_map/all_to_all | solution.py:155
  16.4 26.7 %collective-permute-start.18 = (f32[2,128,1024]{2,1,0:T(8,128)}, f32[2,128,1024]{2,1,0:T(8,128)}, u32[]{:S(2)}, u32[]{:S(2)}) collective-permute-start(f32[2,128,1024]{2,1,0:T(8,128)} %get-tuple-element.59), channel_id=1, source_target_pairs={{0,3},{1,2},{2,1},{3,0},{4,7},{5,6},{6,5},{7,4},{8,11},{9,10},{10,... | collective-permute-start | bytes 3145736 | tf_op jit(solution)/shard_map/ppermute | solution.py:30
  18.7 46.7 %collective-permute-start.17 = (f32[2,128,1024]{2,1,0:T(8,128)S(1)}, f32[2,128,1024]{2,1,0:T(8,128)}, u32[]{:S(2)}, u32[]{:S(2)}) collective-permute-start(f32[2,128,1024]{2,1,0:T(8,128)S(1)} %get-tuple-element.57), channel_id=1, source_target_pairs={{0,2},{1,3},{2,0},{3,1},{4,6},{5,7},{6,4},{7,5},{8,10},{9,11},{10,... | collective-permute-start | bytes 3145736 | tf_op jit(solution)/shard_map/ppermute | solution.py:30
  18.9 46.5 %collective-permute-start.16 = (f32[2,128,1024]{2,1,0:T(8,128)S(1)}, f32[2,128,1024]{2,1,0:T(8,128)}, u32[]{:S(2)}, u32[]{:S(2)}) collective-permute-start(f32[2,128,1024]{2,1,0:T(8,128)S(1)} %get-tuple-element.58), channel_id=1, source_target_pairs={{0,1},{1,0},{2,3},{3,2},{4,5},{5,4},{6,7},{7,6},{8,9},{9,8},{10,11... | collective-permute-start | bytes 3145736 | tf_op jit(solution)/shard_map/ppermute | solution.py:30
  127.2 12.8 %copy-start.6 = (f32[64,64]{1,0:T(8,128)S(1)}, f32[64,64]{1,0:T(8,128)}, u32[]{:S(2)}) copy-start(f32[64,64]{1,0:T(8,128)} %copy.223) | copy-start | bytes 49156
  127.2 12.8 %copy-start.8 = (f32[64,64]{1,0:T(8,128)S(1)}, f32[64,64]{1,0:T(8,128)}, u32[]{:S(2)}) copy-start(f32[64,64]{1,0:T(8,128)} %copy.247) | copy-start | bytes 49156
  152.0 27.4 %slice-start.2 = ((s8[8388608]{0:T(1024)(128)(4,1)}), s8[4194304]{0:T(1024)(128)(4,1)S(1)}, s32[]{:S(2)}) async-start(s8[8388608]{0:T(1024)(128)(4,1)} %bitcast.240), calls=%async_computation.7 | async-start | bytes 8388608
  160.4 19.1 %slice-start.3 = ((s8[8388608]{0:T(1024)(128)(4,1)}), s8[4194304]{0:T(1024)(128)(4,1)S(1)}, s32[]{:S(2)}) async-start(s8[8388608]{0:T(1024)(128)(4,1)} %bitcast.240), calls=%async_computation.8 | async-start | bytes 8388608
  216.3 96.4 %all-to-all-start.2 = ((f32[2,4096,128]{2,0,1:T(2,128)}), f32[2,4096,128]{2,0,1:T(2,128)}, u32[]{:S(2)}, u32[]{:S(2)}) async-start(f32[2,4096,128]{2,0,1:T(2,128)} %copy.253), calls=%async_computation.2 | async-start | bytes 8388608 | tf_op jit(solution)/shard_map/all_to_all | solution.py:191
  330.1 65.5 %all-to-all-start.3 = ((f32[2,512,1024]{2,0,1:T(2,128)}), f32[2,512,1024]{2,0,1:T(2,128)}, u32[]{:S(2)}, u32[]{:S(2)}) async-start(f32[2,512,1024]{2,0,1:T(2,128)} %copy.256), calls=%async_computation.3 | async-start | bytes 8388608 | tf_op jit(solution)/shard_map/all_to_all | solution.py:196
  363.7 46.1 %collective-permute-start = (f32[2,1,1024]{2,0,1:T(2,128)S(1)}, f32[2,1,1024]{2,0,1:T(2,128)S(1)}, u32[]{:S(2)}, u32[]{:S(2)}) collective-permute-start(f32[2,1,1024]{2,0,1:T(2,128)S(1)} %copy.190), channel_id=1, source_target_pairs={{4,0},{8,4},{12,8},{16,12},{20,16},{24,20},{28,24},{5,1},{9,5},{13... | collective-permute-start | bytes 24584 | tf_op jit(solution)/shard_map/ppermute | solution.py:45
  367.7 42.4 %collective-permute-start.1 = (f32[2,1,1024]{2,0,1:T(2,128)}, f32[2,1,1024]{2,0,1:T(2,128)}, u32[]{:S(2)}, u32[]{:S(2)}) collective-permute-start(f32[2,1,1024]{2,0,1:T(2,128)} %copy.192), channel_id=1, source_target_pairs={{0,4},{4,8},{8,12},{12,16},{16,20},{20,24},{24,28},{1,5},{5,9},{9,... | collective-permute-start | bytes 24584 | tf_op jit(solution)/shard_map/ppermute | solution.py:43
  395.6 216.9 %all-to-all-start.1 = ((f32[2,4096,128]{2,0,1:T(2,128)}), f32[2,4096,128]{2,0,1:T(2,128)}, u32[]{:S(2)}, u32[]{:S(2)}) async-start(f32[2,4096,128]{2,0,1:T(2,128)} %copy.235), calls=%async_computation.1 | async-start | bytes 8388608 | tf_op jit(solution)/shard_map/all_to_all | solution.py:192
  413.6 17.4 %collective-permute-start.3 = (f32[2,514,1]{1,2,0:T(1,128)}, f32[2,514,1]{1,2,0:T(1,128)S(1)}, u32[]{:S(2)}, u32[]{:S(2)}) collective-permute-start(f32[2,514,1]{1,2,0:T(1,128)} %get-tuple-element.47), channel_id=1, source_target_pairs={{0,1},{1,2},{2,3},{4,5},{5,6},{6,7},{8,9},{9,10},{10,11},{12,13},{... | collective-permute-start | bytes 12344 | tf_op jit(solution)/shard_map/ppermute | solution.py:43
  418.0 13.0 %collective-permute-start.2 = (f32[2,514,1]{1,2,0:T(1,128)}, f32[2,514,1]{1,2,0:T(1,128)S(1)}, u32[]{:S(2)}, u32[]{:S(2)}) collective-permute-start(f32[2,514,1]{1,2,0:T(1,128)} %get-tuple-element.46), channel_id=1, source_target_pairs={{1,0},{2,1},{3,2},{5,4},{6,5},{7,6},{9,8},{10,9},{11,10},{13,12},{... | collective-permute-start | bytes 12344 | tf_op jit(solution)/shard_map/ppermute | solution.py:45
  451.5 42.0 %collective-permute-start.4 = (f32[2,1,1024]{2,0,1:T(2,128)}, f32[2,1,1024]{2,0,1:T(2,128)}, u32[]{:S(2)}, u32[]{:S(2)}) collective-permute-start(f32[2,1,1024]{2,0,1:T(2,128)} %copy.199), channel_id=1, source_target_pairs={{4,0},{8,4},{12,8},{16,12},{20,16},{24,20},{28,24},{5,1},{9,5},{13... | collective-permute-start | bytes 24584 | tf_op jit(solution)/shard_map/ppermute | solution.py:45
  456.7 39.4 %collective-permute-start.5 = (f32[2,1,1024]{2,0,1:T(2,128)}, f32[2,1,1024]{2,0,1:T(2,128)}, u32[]{:S(2)}, u32[]{:S(2)}) collective-permute-start(f32[2,1,1024]{2,0,1:T(2,128)} %copy.201), channel_id=1, source_target_pairs={{0,4},{4,8},{8,12},{12,16},{16,20},{20,24},{24,28},{1,5},{5,9},{9,... | collective-permute-start | bytes 24584 | tf_op jit(solution)/shard_map/ppermute | solution.py:43
  499.9 117.6 %collective-permute-start.7 = (f32[2,514,1]{1,2,0:T(1,128)}, f32[2,514,1]{1,2,0:T(1,128)}, u32[]{:S(2)}, u32[]{:S(2)}) collective-permute-start(f32[2,514,1]{1,2,0:T(1,128)} %get-tuple-element.45), channel_id=1, source_target_pairs={{0,1},{1,2},{2,3},{4,5},{5,6},{6,7},{8,9},{9,10},{10,11},{12,13},{... | collective-permute-start | bytes 12344 | tf_op jit(solution)/shard_map/ppermute | solution.py:43
  503.9 113.6 %collective-permute-start.6 = (f32[2,514,1]{1,2,0:T(1,128)}, f32[2,514,1]{1,2,0:T(1,128)}, u32[]{:S(2)}, u32[]{:S(2)}) collective-permute-start(f32[2,514,1]{1,2,0:T(1,128)} %get-tuple-element.44), channel_id=1, source_target_pairs={{1,0},{2,1},{3,2},{5,4},{6,5},{7,6},{9,8},{10,9},{11,10},{13,12},{... | collective-permute-start | bytes 12344 | tf_op jit(solution)/shard_map/ppermute | solution.py:45
  546.5 20.1 %slice-start = ((s8[8388608]{0:T(1024)(128)(4,1)}), s8[4194304]{0:T(1024)(128)(4,1)S(1)}, s32[]{:S(2)}) async-start(s8[8388608]{0:T(1024)(128)(4,1)} %bitcast.237), calls=%async_computation.5 | async-start | bytes 8388608
  550.6 16.0 %slice-start.1 = ((s8[8388608]{0:T(1024)(128)(4,1)}), s8[4194304]{0:T(1024)(128)(4,1)S(1)}, s32[]{:S(2)}) async-start(s8[8388608]{0:T(1024)(128)(4,1)} %bitcast.237), calls=%async_computation.6 | async-start | bytes 8388608
  550.6 16.0 %copy-start.7 = (f32[64,64]{1,0:T(8,128)S(1)}, f32[64,64]{1,0:T(8,128)}, u32[]{:S(2)}) copy-start(f32[64,64]{1,0:T(8,128)} %copy.223) | copy-start | bytes 49156
  550.6 16.0 %copy-start.9 = (f32[64,64]{1,0:T(8,128)S(1)}, f32[64,64]{1,0:T(8,128)}, u32[]{:S(2)}) copy-start(f32[64,64]{1,0:T(8,128)} %copy.246) | copy-start | bytes 49156
  612.5 109.2 %all-to-all-start.4 = ((f32[2,128,4096]{1,0,2:T(2,128)}), f32[2,128,4096]{1,0,2:T(2,128)}, u32[]{:S(2)}, u32[]{:S(2)}) async-start(f32[2,128,4096]{1,0,2:T(2,128)} %copy.267), calls=%async_computation.4 | async-start | bytes 8388608 | tf_op jit(solution)/shard_map/all_to_all | solution.py:207
  652.3 7.4 collective-permute-start.8
  657.7 5.3 collective-permute-start.9
  665.2 9.9 %collective-permute-start.11 = (f32[2,514,1]{1,2,0:T(1,128)S(1)}, f32[2,514,1]{1,2,0:T(1,128)S(1)}, u32[]{:S(2)}, u32[]{:S(2)}) collective-permute-start(f32[2,514,1]{1,2,0:T(1,128)S(1)} %get-tuple-element.43), channel_id=1, source_target_pairs={{0,1},{1,2},{2,3},{4,5},{5,6},{6,7},{8,9},{9,10},{10,11},{12,13},{... | collective-permute-start | bytes 12344 | tf_op jit(solution)/shard_map/ppermute | solution.py:43
  670.3 4.9 collective-permute-start.10
  695.1 5.6 collective-permute-start.12
  697.4 5.3 collective-permute-start.13
  704.9 32.0 %collective-permute-start.15 = (f32[2,514,1]{1,2,0:T(1,128)S(1)}, f32[2,514,1]{1,2,0:T(1,128)S(1)}, u32[]{:S(2)}, u32[]{:S(2)}) collective-permute-start(f32[2,514,1]{1,2,0:T(1,128)S(1)} %get-tuple-element.41), channel_id=1, source_target_pairs={{0,1},{1,2},{2,3},{4,5},{5,6},{6,7},{8,9},{9,10},{10,11},{12,13},{... | collective-permute-start | bytes 12344 | tf_op jit(solution)/shard_map/ppermute | solution.py:43
  709.6 27.3 %collective-permute-start.14 = (f32[2,514,1]{1,2,0:T(1,128)S(1)}, f32[2,514,1]{1,2,0:T(1,128)S(1)}, u32[]{:S(2)}, u32[]{:S(2)}) collective-permute-start(f32[2,514,1]{1,2,0:T(1,128)S(1)} %get-tuple-element.40), channel_id=1, source_target_pairs={{1,0},{2,1},{3,2},{5,4},{6,5},{7,6},{9,8},{10,9},{11,10},{13,12},{... | collective-permute-start | bytes 12344 | tf_op jit(solution)/shard_map/ppermute | solution.py:45
  (6 other events, 20.7 us)
